TPU v7x, 32 devices: a whole 2x2x4 slice. The times are simulated.
32 devices in a mesh: tm: 4 (over x, core), firm: 8 (over z, y).
Axes of the slice: x: 2, y: 2, z: 4, core: 2. Of those that a mesh axis runs over, the one named last changes fastest.
Arguments:
- features: bfloat16 [32, 2048, 256], P('tm', 'firm'), may hold values from -6 to 6
- supply_counts: int32 [32, 2048, 3, 256], P('tm', 'firm'), may hold values from 0 to 3
- bank_ids: int32 [32, 2048], P('tm', 'firm'), may hold values from 0 to 63
- sector_ids: int32 [32, 2048], P('tm', 'firm'), may hold values from 0 to 31
- bank_table: bfloat16 [64, 256], P('firm'), may hold values from -6 to 6
- sector_table: bfloat16 [32, 256], P('firm'), may hold values from -6 to 6
- w_supply: bfloat16 [256, 256], replicated, may hold values from -0.375 to 0.375
- w_query: bfloat16 [256, 256], replicated, may hold values from -0.375 to 0.375
- w_key: bfloat16 [256, 256], replicated, may hold values from -0.375 to 0.375
- w_value: bfloat16 [256, 256], replicated, may hold values from -0.375 to 0.375
- w_out: bfloat16 [256, 256], replicated, may hold values from -0.375 to 0.375
- w_in: bfloat16 [256, 1024], replicated, may hold values from -0.375 to 0.375
- w_down: bfloat16 [1024, 256], replicated, may hold values from -0.1875 to 0.1875
- gain_mix: float32 [256], replicated, may hold values from 0.1 to 1.9
- gain_ffn: float32 [256], replicated, may hold values from 0.1 to 1.9
Outputs:
- result: bfloat16 [32, 2048, 256], P('tm', 'firm')
All inputs are finite; a program needn't handle non-finite values.
Results may differ from a plain program's by a relative error of at most 0.0059.
Values may be sent and summed in bfloat16 or wider, within the bound.
A program may use at most 64 MiB of HBM per device.

v0:
```python
import jax
import jax.numpy as jnp
from jax import lax
from jax.sharding import PartitionSpec as P

HEADS = 4


def padded(x, sides, width):
    for axis, dim in sides:
        devices, length = (lax.axis_size(axis), x.shape[dim])
        up = [(i, (i + 1) % devices) for i in range(devices - 1)]
        down = [(j, i) for i, j in up]
        last = lax.slice_in_dim(x, length - width, length, axis=dim)
        leading = lax.slice_in_dim(x, 0, width, axis=dim)
        before = lax.ppermute(last, axis, up)
        after = lax.ppermute(leading, axis, down)
        x = jnp.concatenate([before, x, after], axis=dim)
    return x


def from_behind(x, axis, by):
    devices = lax.axis_size(axis)
    pairs = [(i, i + by) for i in range(devices) if 0 <= i + by < devices]
    return lax.ppermute(x, axis, pairs)


def rms_norm(values, gain):
    scale = lax.rsqrt(jnp.mean(values * values, axis=-1, keepdims=True) + 1e-06)
    return values * scale * gain


def body(
    features,
    supply_counts,
    bank_ids,
    sector_ids,
    bank_table,
    sector_table,
    w_supply,
    w_query,
    w_key,
    w_value,
    w_out,
    w_in,
    w_down,
    gain_mix,
    gain_ffn,
):
    months, firms, width = features.shape
    rows = months * firms
    flat = features.reshape(rows, width)
    supplied = (
        jnp.dot(flat, w_supply, preferred_element_type=jnp.float32)
        .astype(jnp.bfloat16)
        .reshape(months, firms, width)
    )
    extended = padded(supplied, (("firm", 1),), firms)
    tiles = supply_counts.reshape(months, firms, 3 * firms).astype(jnp.bfloat16)
    degree = 1.0 + jnp.sum(supply_counts, axis=(2, 3)).astype(jnp.float32)
    message = jnp.einsum("mfs,msd->mfd", tiles, extended, preferred_element_type=jnp.float32)
    message = message * lax.rsqrt(degree)[..., None]
    bank_local = bank_table.shape[0]
    sector_local = sector_table.shape[0]
    per_owner = bank_local + sector_local
    hub_local = jnp.concatenate([bank_table, sector_table], axis=0)
    bank_flat = bank_ids.reshape(rows)
    sector_flat = sector_ids.reshape(rows)
    bank_pos = bank_flat // bank_local * per_owner + bank_flat % bank_local
    sector_pos = sector_flat // sector_local * per_owner + bank_local + sector_flat % sector_local
    hub_whole = lax.all_gather(hub_local, "firm", axis=0, tiled=True)
    hubs = jnp.take(hub_whole, bank_pos, axis=0).astype(jnp.float32) + jnp.take(
        hub_whole, sector_pos, axis=0
    ).astype(jnp.float32)
    mixed = flat.astype(jnp.float32) + message.reshape(rows, width) + hubs
    normed = rms_norm(mixed, gain_mix).astype(jnp.bfloat16)
    query = (
        jnp.dot(normed, w_query, preferred_element_type=jnp.float32)
        .astype(jnp.bfloat16)
        .reshape(months, firms, width)
    )
    key = (
        jnp.dot(normed, w_key, preferred_element_type=jnp.float32)
        .astype(jnp.bfloat16)
        .reshape(months, firms, width)
    )
    value = (
        jnp.dot(normed, w_value, preferred_element_type=jnp.float32)
        .astype(jnp.bfloat16)
        .reshape(months, firms, width)
    )
    earlier_key, earlier_value = from_behind((key, value), "tm", 1)
    earlier_key = earlier_key[months - 3 :]
    earlier_value = earlier_value[months - 3 :]
    keys_all = jnp.concatenate([earlier_key, key], axis=0)
    values_all = jnp.concatenate([earlier_value, value], axis=0)
    heads = HEADS
    head_size = width // heads
    query4 = query.reshape(months, firms, heads, head_size)
    first_month = lax.axis_index("tm") * months
    month_local = lax.iota(jnp.int32, months)
    total = jnp.zeros((months, firms, heads, head_size), jnp.float32)
    for lag in range(4):
        key_l = keys_all[3 - lag : 3 - lag + months].reshape(months, firms, heads, head_size)
        value_l = values_all[3 - lag : 3 - lag + months].reshape(months, firms, heads, head_size)
        score = jnp.einsum(
            "mfhd,mfhd->mfh", query4, key_l, preferred_element_type=jnp.float32
        ) / jnp.sqrt(jnp.float32(head_size)) - jnp.log(jnp.float32(4.0))
        valid = (first_month + month_local - lag >= 0).astype(jnp.float32)[:, None, None]
        total = total + (jax.nn.sigmoid(score) * valid)[..., None] * value_l.astype(jnp.float32)
    attended = total.astype(jnp.bfloat16).reshape(rows, width)
    second = mixed + jnp.dot(attended, w_out, preferred_element_type=jnp.float32)
    normed2 = rms_norm(second, gain_ffn).astype(jnp.bfloat16)
    inner = jax.nn.gelu(jnp.dot(normed2, w_in, preferred_element_type=jnp.float32)).astype(
        jnp.bfloat16
    )
    final = second + jnp.dot(inner, w_down, preferred_element_type=jnp.float32)
    return final.astype(jnp.bfloat16).reshape(months, firms, width)


def solution(mesh):
    in_specs = (
        P("tm", "firm", None),
        P("tm", "firm", None, None),
        P("tm", "firm"),
        P("tm", "firm"),
        P("firm", None),
        P("firm", None),
        P(),
        P(),
        P(),
        P(),
        P(),
        P(),
        P(),
        P(),
        P(),
    )
    out_specs = P("tm", "firm", None)
    return jax.shard_map(body, mesh=mesh, in_specs=in_specs, out_specs=out_specs, check_vma=False)
```

profile of v0, /device:TPU:0, one launch (start us, length us, event | category | flops | bytes accessed | tf_op | source)
XLA Modules:
  0.0 171.3 jit_solution(2763451654830238360)
XLA Ops:
  0.0 1.7 convolution_convert_fusion.3
  1.7 1.3 collective-permute-start.1
  3.0 6.5 %collective-permute-start = (bf16[8,256,256]{2,1,0:T(8,128)(2,1)S(1)}, bf16[8,256,256]{2,1,0:T(8,128)(2,1)}, u32[]{:S(2)}, u32[]{:S(2)}) collective-permute-start(bf16[8,256,256]{2,1,0:T(8,128)(2,1)S(1)} %bitcast.95), channel_id=1, source_target_pairs={{0,1},{1,2},{2,3},{3,4},{4,5},{5,6},{6,7},{8,9},{9,10},{10,11},{11... | collective-permute-start | bytes 3145736 | tf_op jit(solution)/shard_map/ppermute | solution.py:16
  9.6 6.6 %copy.26 = s32[8,256,3,256]{1,3,2,0:T(8,128)} copy(s32[8,256,3,256]{3,1,2,0:T(8,128)} %param.18) | data formatting | bytes 12582912 | tf_op args[1]
  16.2 3.1 %reduce_sum.27 = s32[8,256]{1,0:T(8,128)S(1)} reduce(s32[8,256,3,256]{3,1,2,0:T(8,128)} %param.18, s32[]{:T(128)} %constant.84.clone.1), dimensions={2,3}, to_apply=%region_0.0 | reduce | flops 1570816 | bytes 6299652 | tf_op jit(solution)/shard_map/reduce_sum | solution.py:60
  19.3 57.3 %all-gather = bf16[8,12,256]{2,1,0:T(8,128)(2,1)S(1)} all-gather(bf16[1,12,256]{2,1,0:T(8,128)(2,1)S(1)} %maximum_bitcast_fusion), channel_id=1, replica_groups=mesh['tm'=4,'firm'=8] {'firm'}, dimensions={0}, use_global_device_ids=true | all-gather | bytes 55296 | tf_op jit(solution)/shard_map/all_gather | solution.py:71
  76.7 9.1 %gather_fusion.1 = bf16[2048,256]{1,0:T(8,128)(2,1)} fusion(bf16[96,256]{1,0:T(8,128)(2,1)S(1)} %reshape.138, s32[2048]{0:T(1024)S(1)} %broadcast_clamp_fusion), kind=kCustom, calls=%fused_computation.1.clone | custom fusion | bytes 2105344 | tf_op jit(solution)/shard_map/jit(_take)/gather | solution.py:72
  85.8 9.0 %gather_fusion = bf16[2048,256]{1,0:T(8,128)(2,1)} fusion(bf16[96,256]{1,0:T(8,128)(2,1)S(1)} %reshape.138, s32[2048]{0:T(1024)S(1)} %broadcast_clamp_fusion.1), kind=kCustom, calls=%fused_computation.clone | custom fusion | bytes 2105344 | tf_op jit(solution)/shard_map/jit(_take)/gather | solution.py:72
  94.8 5.2 %convert_element_type.105 = bf16[8,256,3,256]{1,3,2,0:T(8,128)(2,1)} convert(s32[8,256,3,256]{1,3,2,0:T(8,128)} %copy.26) | non-fusion elementwise | flops 1572864 | bytes 9437184 | tf_op jit(solution)/shard_map/convert_element_type | solution.py:59
  100.0 3.8 %fusion.29 = f32[8,256,256]{1,2,0:T(8,128)S(1)} fusion(bf16[8,256,768]{1,2,0:T(8,128)(2,1)} %bitcast.93, bf16[8,256,256]{2,1,0:T(8,128)(2,1)} %collective-permute-done.1, bf16[8,256,256]{2,1,0:T(8,128)(2,1)S(1)} %bitcast.96, bf16[8,256,256]{2,1,0:T(8,128)(2,1)} %collective-permute-done, f32[8,256]{1,0:T(8,128)S(1)} %add_rsqrt_fusion.2), kind=kOutput, calls=%fused_computation.47 | convolution fusion | flops 815267840 | bytes 8396800 | tf_op jit(solution)/shard_map/mfs,msd->mfd/dot_general | solution.py:61
  103.9 2.1 %multiply_reduce_fusion.5 = (f32[2048]{0:T(1024)S(1)}, f32[2048,256]{1,0:T(8,128)S(1)}) fusion(bf16[2048,256]{1,0:T(8,128)(2,1)S(1)} %copy-done.8, pred[2048]{0:T(1024)(128)(4,1)S(1)} %get-tuple-element.13, bf16[2048,256]{1,0:T(8,128)(2,1)S(1)} %copy-done.9, pred[2048]{0:T(1024)(128)(4,1)S(1)} %get-tuple-element.23, f32[8,256,256]{1,2,0:T(8,128)S(1)} %fusion.29, ...), kind=kLoop, calls=%fused_computation.42 | loop fusion | flops 5240832 | bytes 7352320 | tf_op jit(solution)/shard_map/reduce_sum | solution.py:29
  106.1 0.3 multiply_convert_fusion.3
  106.5 1.0 copy-done.1
  107.4 1.4 convolution_convert_fusion.1
  108.9 2.3 %copy.31 = bf16[8,256,256]{1,2,0:T(8,128)(2,1)} copy(bf16[8,256,256]{2,1,0:T(8,128)(2,1)} %bitcast.77) | data formatting | bytes 2097152 | tf_op jit(solution)/shard_map/reshape | solution.py:85
  111.1 2.3 %collective-permute-start.2 = (bf16[8,256,256]{1,2,0:T(8,128)(2,1)}, bf16[8,256,256]{1,2,0:T(8,128)(2,1)}, u32[]{:S(2)}, u32[]{:S(2)}) collective-permute-start(bf16[8,256,256]{1,2,0:T(8,128)(2,1)} %copy.31), channel_id=1, source_target_pairs={{0,8},{8,16},{16,24},{1,9},{9,17},{17,25},{2,10},{10,18},{18,26},{... | collective-permute-start | bytes 3145736 | tf_op jit(solution)/shard_map/ppermute | solution.py:25
  113.5 2.3 %copy.29 = bf16[2048,256]{0,1:T(8,128)(2,1)} copy(bf16[2048,256]{1,0:T(8,128)(2,1)} %convolution_convert_fusion.1) | data formatting | bytes 2097152 | tf_op jit(solution)/shard_map/convert_element_type | solution.py:84
  115.7 2.7 %convolution_convert_fusion.2 = bf16[2048,256]{1,0:T(8,128)(2,1)} fusion(bf16[2048,256]{1,0:T(8,128)(2,1)} %copy-done.1, bf16[256,256]{1,0:T(8,128)(2,1)S(1)} %copy-done.12), kind=kOutput, calls=%fused_computation.24 | convolution fusion | flops 268959744 | bytes 2228224 | tf_op jit(solution)/shard_map/dot_general | solution.py:78
  118.4 2.3 %copy.28 = bf16[2048,256]{0,1:T(8,128)(2,1)} copy(bf16[2048,256]{1,0:T(8,128)(2,1)} %convolution_convert_fusion.2) | data formatting | bytes 2097152 | tf_op jit(solution)/shard_map/convert_element_type | solution.py:79
  120.7 1.6 copy.59
  122.3 0.3 copy.60
  122.6 1.5 convert.11
  124.2 1.4 convolution_convert_fusion
  125.6 4.1 %collective-permute-start.3 = (bf16[8,256,256]{2,1,0:T(8,128)(2,1)}, bf16[8,256,256]{2,1,0:T(8,128)(2,1)}, u32[]{:S(2)}, u32[]{:S(2)}) collective-permute-start(bf16[8,256,256]{2,1,0:T(8,128)(2,1)} %bitcast.8), channel_id=1, source_target_pairs={{0,8},{8,16},{16,24},{1,9},{9,17},{17,25},{2,10},{10,18},{18,26},{... | collective-permute-start | bytes 3145736 | tf_op jit(solution)/shard_map/ppermute | solution.py:25
  129.7 0.3 multiply_reduce_fusion.3
  129.9 0.1 divide_multiply_fusion
  130.0 0.1 mul.168
  130.2 2.2 %copy.61 = f32[32,8,8,256]{3,1,2,0:T(8,128)} copy(f32[32,8,8,256]{3,2,1,0:T(8,128)S(1)} %bitcast.78) | data formatting | bytes 4194304
  132.4 2.9 %copy.30 = f32[2048,256]{1,0:T(8,128)} copy(f32[2048,256]{0,1:T(8,128)} %bitcast.79) | data formatting | bytes 4194304 | tf_op jit(solution)/shard_map/mul | solution.py:110
  135.3 1.0 slice.36
  136.3 2.2 %fusion.34 = (bf16[8,256,256]{1,2,0:T(8,128)(2,1)S(1)}, bf16[8,256,256]{1,2,0:T(8,128)(2,1)S(1)}, bf16[8,256,256]{1,2,0:T(8,128)(2,1)S(1)}) fusion(bf16[8,256,256]{1,2,0:T(8,128)(2,1)} %copy.31, bf16[3,256,256]{1,2,0:T(8,128)(2,1)S(1)} %slice.36), kind=kLoop, calls=%fused_computation.54 | loop fusion | flops 1572864 | bytes 4587520 | tf_op jit(solution)/shard_map/concatenate | solution.py:95
  138.5 0.1 copy-done.3
  138.6 1.4 multiply_reduce_fusion.2
  140.1 0.1 mul.178
  140.2 2.2 %copy.63 = f32[32,8,8,256]{3,1,2,0:T(8,128)} copy(f32[32,8,8,256]{3,2,1,0:T(8,128)S(1)} %bitcast.80) | data formatting | bytes 4194304
  142.4 2.9 %copy.34 = f32[2048,256]{1,0:T(8,128)} copy(f32[2048,256]{0,1:T(8,128)} %bitcast.81) | data formatting | bytes 4194304 | tf_op jit(solution)/shard_map/mul | solution.py:110
  145.4 0.1 mul.183
  145.6 2.2 %copy.64 = f32[32,8,8,256]{3,1,2,0:T(8,128)} copy(f32[32,8,8,256]{3,2,1,0:T(8,128)S(1)} %bitcast.82) | data formatting | bytes 4194304
  147.8 2.9 %copy.35 = f32[2048,256]{1,0:T(8,128)} copy(f32[2048,256]{0,1:T(8,128)} %bitcast.83) | data formatting | bytes 4194304 | tf_op jit(solution)/shard_map/mul | solution.py:110
  150.7 0.1 mul.173
  150.9 2.2 %copy.62 = f32[32,8,8,256]{3,1,2,0:T(8,128)} copy(f32[32,8,8,256]{3,2,1,0:T(8,128)S(1)} %bitcast.84) | data formatting | bytes 4194304
  153.1 2.9 %copy.33 = f32[2048,256]{1,0:T(8,128)} copy(f32[2048,256]{0,1:T(8,128)} %bitcast.85) | data formatting | bytes 4194304 | tf_op jit(solution)/shard_map/mul | solution.py:110
  156.1 1.0 slice.39
  157.1 2.0 %fusion.33 = (bf16[8,256,256]{2,1,0:T(8,128)(2,1)S(1)}, bf16[8,256,256]{2,1,0:T(8,128)(2,1)S(1)}, bf16[8,256,256]{2,1,0:T(8,128)(2,1)S(1)}) fusion(bf16[8,256,256]{2,1,0:T(8,128)(2,1)} %bitcast.8, bf16[3,256,256]{2,1,0:T(8,128)(2,1)S(1)} %slice.39), kind=kLoop, calls=%fused_computation.53 | loop fusion | flops 1572864 | bytes 4587520 | tf_op jit(solution)/shard_map/concatenate | solution.py:96
  159.2 0.2 copy-done.4
  159.4 0.6 copy-done.5
  160.0 4.9 %multiply_reduce_fusion.4 = (f32[2048]{0:T(1024)S(1)}, f32[2048,256]{1,0:T(8,128)}) fusion(f32[2048,256]{1,0:T(8,128)S(1)} %get-tuple-element.10, bf16[256,256]{1,0:T(8,128)(2,1)S(1)} %copy-done.10, f32[2048,256]{1,0:T(8,128)} %copy.35, bf16[2048,256]{1,0:T(8,128)(2,1)S(1)} %bitcast.91, f32[2048,256]{1,0:T(8,128)S(1)} %copy-done.5, ...), kind=kOutput, calls=%fused_computation.40 | convolution fusion | flops 276297728 | bytes 16916480 | tf_op jit(solution)/shard_map/dot_general | solution.py:112
  165.0 6.4 %fusion.21 = bf16[2048,256]{1,0:T(8,128)(2,1)} fusion(f32[2048,256]{1,0:T(8,128)} %get-tuple-element.22, bf16[1024,256]{1,0:T(8,128)(2,1)S(1)} %copy-done, bf16[256,1024]{1,0:T(8,128)(2,1)S(1)} %copy-done.19, f32[256]{0:T(256)S(1)} %copy-done.20, f32[2048]{0:T(1024)S(1)} %add_rsqrt_fusion), kind=kOutput, calls=%fused_computation.21 | convolution fusion | flops 2168979456 | bytes 4203520 | tf_op jit(solution)/shard_map/dot_general | solution.py:117
  (57 shorter events, 0.4 us)
Async XLA Ops:
  0.0 165.0 %copy-start = (bf16[1024,256]{1,0:T(8,128)(2,1)S(1)}, bf16[1024,256]{1,0:T(8,128)(2,1)}, u32[]{:S(2)}) copy-start(bf16[1024,256]{1,0:T(8,128)(2,1)} %param.29) | copy-start | bytes 1572868
  0.0 9.5 %copy-start.17 = (bf16[4,256]{1,0:T(4,128)(2,1)S(1)}, bf16[4,256]{1,0:T(4,128)(2,1)}, u32[]{:S(2)}) copy-start(bf16[4,256]{1,0:T(4,128)(2,1)} %param.22) | copy-start | bytes 6148
  0.0 9.5 %copy-start.16 = (bf16[8,256]{1,0:T(8,128)(2,1)S(1)}, bf16[8,256]{1,0:T(8,128)(2,1)}, u32[]{:S(2)}) copy-start(bf16[8,256]{1,0:T(8,128)(2,1)} %param.21) | copy-start | bytes 12292
  0.0 9.6 %copy-start.14 = (s32[8,256]{1,0:T(8,128)S(1)}, s32[8,256]{1,0:T(8,128)}, u32[]{:S(2)}) copy-start(s32[8,256]{1,0:T(8,128)} %param.19) | copy-start | bytes 24580
  0.0 9.6 %copy-start.15 = (s32[8,256]{1,0:T(8,128)S(1)}, s32[8,256]{1,0:T(8,128)}, u32[]{:S(2)}) copy-start(s32[8,256]{1,0:T(8,128)} %param.20) | copy-start | bytes 24580
  1.7 98.2 %collective-permute-start.1 = (bf16[8,256,256]{2,1,0:T(8,128)(2,1)S(1)}, bf16[8,256,256]{2,1,0:T(8,128)(2,1)}, u32[]{:S(2)}, u32[]{:S(2)}) collective-permute-start(bf16[8,256,256]{2,1,0:T(8,128)(2,1)S(1)} %bitcast.94), channel_id=1, source_target_pairs={{1,0},{2,1},{3,2},{4,3},{5,4},{6,5},{7,6},{9,8},{10,9},{11,10},{12... | collective-permute-start | bytes 3145736 | tf_op jit(solution)/shard_map/ppermute | solution.py:17
  3.0 97.0 %collective-permute-start = (bf16[8,256,256]{2,1,0:T(8,128)(2,1)S(1)}, bf16[8,256,256]{2,1,0:T(8,128)(2,1)}, u32[]{:S(2)}, u32[]{:S(2)}) collective-permute-start(bf16[8,256,256]{2,1,0:T(8,128)(2,1)S(1)} %bitcast.95), channel_id=1, source_target_pairs={{0,1},{1,2},{2,3},{3,4},{4,5},{5,6},{6,7},{8,9},{9,10},{10,11},{11... | collective-permute-start | bytes 3145736 | tf_op jit(solution)/shard_map/ppermute | solution.py:16
  100.0 3.9 %copy-start.7 = (bf16[8,256,256]{2,1,0:T(8,128)(2,1)S(1)}, bf16[8,256,256]{2,1,0:T(8,128)(2,1)}, u32[]{:S(2)}) copy-start(bf16[8,256,256]{2,1,0:T(8,128)(2,1)} %param.17) | copy-start | bytes 3145732
  100.0 3.9 %copy-start.8 = (bf16[2048,256]{1,0:T(8,128)(2,1)S(1)}, bf16[2048,256]{1,0:T(8,128)(2,1)}, u32[]{:S(2)}) copy-start(bf16[2048,256]{1,0:T(8,128)(2,1)} %gather_fusion.1) | copy-start | bytes 3145732
  100.0 3.9 %copy-start.9 = (bf16[2048,256]{1,0:T(8,128)(2,1)S(1)}, bf16[2048,256]{1,0:T(8,128)(2,1)}, u32[]{:S(2)}) copy-start(bf16[2048,256]{1,0:T(8,128)(2,1)} %gather_fusion) | copy-start | bytes 3145732
  103.9 2.2 %copy-start.18 = (f32[256]{0:T(256)S(1)}, f32[256]{0:T(256)}, u32[]{:S(2)}) copy-start(f32[256]{0:T(256)} %param.30) | copy-start | bytes 3076
  106.1 1.4 copy-start.11
  106.4 1.0 copy-start.1
  108.9 6.9 %copy-start.12 = (bf16[256,256]{1,0:T(8,128)(2,1)S(1)}, bf16[256,256]{1,0:T(8,128)(2,1)}, u32[]{:S(2)}) copy-start(bf16[256,256]{1,0:T(8,128)(2,1)} %param.24) | copy-start | bytes 393220
  111.1 24.1 %collective-permute-start.2 = (bf16[8,256,256]{1,2,0:T(8,128)(2,1)}, bf16[8,256,256]{1,2,0:T(8,128)(2,1)}, u32[]{:S(2)}, u32[]{:S(2)}) collective-permute-start(bf16[8,256,256]{1,2,0:T(8,128)(2,1)} %copy.31), channel_id=1, source_target_pairs={{0,8},{8,16},{16,24},{1,9},{9,17},{17,25},{2,10},{10,18},{18,26},{... | collective-permute-start | bytes 3145736 | tf_op jit(solution)/shard_map/ppermute | solution.py:25
  120.7 1.6 copy-start.6
  122.6 1.5 copy-start.2
  122.6 1.5 copy-start.13
  125.6 30.5 %collective-permute-start.3 = (bf16[8,256,256]{2,1,0:T(8,128)(2,1)}, bf16[8,256,256]{2,1,0:T(8,128)(2,1)}, u32[]{:S(2)}, u32[]{:S(2)}) collective-permute-start(bf16[8,256,256]{2,1,0:T(8,128)(2,1)} %bitcast.8), channel_id=1, source_target_pairs={{0,8},{8,16},{16,24},{1,9},{9,17},{17,25},{2,10},{10,18},{18,26},{... | collective-permute-start | bytes 3145736 | tf_op jit(solution)/shard_map/ppermute | solution.py:25
  136.3 2.3 %copy-start.3 = (f32[8,256,4,64]{1,0,3,2:T(8,128)S(1)}, f32[8,256,4,64]{1,0,3,2:T(8,128)}, u32[]{:S(2)}) copy-start(f32[8,256,4,64]{1,0,3,2:T(8,128)} %convert.11) | copy-start | bytes 6291460
  157.1 2.3 %copy-start.4 = (f32[2048,256]{1,0:T(8,128)S(1)}, f32[2048,256]{1,0:T(8,128)}, u32[]{:S(2)}) copy-start(f32[2048,256]{1,0:T(8,128)} %copy.30) | copy-start | bytes 6291460
  157.1 2.9 %copy-start.5 = (f32[2048,256]{1,0:T(8,128)S(1)}, f32[2048,256]{1,0:T(8,128)}, u32[]{:S(2)}) copy-start(f32[2048,256]{1,0:T(8,128)} %copy.34) | copy-start | bytes 6291460
  157.1 2.9 %copy-start.10 = (bf16[256,256]{1,0:T(8,128)(2,1)S(1)}, bf16[256,256]{1,0:T(8,128)(2,1)}, u32[]{:S(2)}) copy-start(bf16[256,256]{1,0:T(8,128)(2,1)} %param.27) | copy-start | bytes 393220
  160.0 4.9 %copy-start.19 = (bf16[256,1024]{1,0:T(8,128)(2,1)S(1)}, bf16[256,1024]{1,0:T(8,128)(2,1)}, u32[]{:S(2)}) copy-start(bf16[256,1024]{1,0:T(8,128)(2,1)} %param.28) | copy-start | bytes 1572868
  160.0 4.9 %copy-start.20 = (f32[256]{0:T(256)S(1)}, f32[256]{0:T(256)}, u32[]{:S(2)}) copy-start(f32[256]{0:T(256)} %param.31) | copy-start | bytes 3076
where the time goes:
time: 172 us; the launch traced here: 171 us
  local copies, waits for them, and re-layouts  58.6 us (34%)
  blocking collectives  57.3 us (33%)
  matrix products  22.3 us (13%)
  other arithmetic  18.5 us (11%)
  starting transfers between devices  14.2 us (8%)
    all_gather x1, blocking collectives, body(): hub_whole = lax.all_gather(hub_local, 'firm', axis=0, tiled=True)  57.3 us
    unnamed x52, local copies, waits for them, and re-layouts  19.4 us
    mul x8, local copies, waits for them, and re-layouts, body(): (jax.nn.sigmoid(score) * valid)[..., None] * value_l.astype(jnp.float32)  12.2 us
    gather x1, local copies, waits for them, and re-layouts, body(): jnp.take(hub_whole, sector_pos, axis=0).astype(jnp.float32)  9.06 us
    gather x1, local copies, waits for them, and re-layouts, body(): jnp.take(hub_whole, bank_pos, axis=0).astype(jnp.float32)  9 us
    ppermute x1, starting transfers between devices, padded(): before = lax.ppermute(last, axis, up)  6.5 us
    ppermute x2, starting transfers between devices, from_behind(): return lax.ppermute(x, axis, pairs)  6.4 us
    dot_general x1, matrix products, body(): final = second + jnp.dot(inner, w_down, preferred_element_type=jnp.float32)  6.36 us
  transfers between devices with their start and end apart: 4, of which 0 were waited for; matrix products, arithmetic and copies ran while one was open for 42% of the time, Pallas kernels for 0%

commit v1 on v0

v1 whole, which is shorter than its diff:
```python
import functools
import math

import jax
import jax.numpy as jnp
from jax import lax
from jax.experimental import pallas as pl
from jax.experimental.pallas import tpu as pltpu
from jax.sharding import PartitionSpec as P

HEADS = 4
LAGS = 3
AHEAD = 3
MESH = pl.DeviceIdType.MESH
F32 = jnp.float32
BF16 = jnp.bfloat16


def dot(a, b):
    return jnp.dot(a, b, preferred_element_type=F32)


def rms_norm(values, gain):
    scale = lax.rsqrt(jnp.mean(values * values, axis=-1, keepdims=True) + 1e-06)
    return values * scale * gain


def kernel(
    groups,
    owners,
    features,
    counts_hbm,
    bank_ids,
    sector_ids,
    bank_table,
    sector_table,
    w_supply,
    w_query,
    w_key,
    w_value,
    w_out,
    w_in,
    w_down,
    gain_mix,
    gain_ffn,
    result,
    counts,
    hub_own,
    hub,
    supplied,
    direct,
    relay,
    normed_out,
    normed_in,
    query,
    key,
    value,
    mixed,
    head_sum,
    counts_sem,
    hub_send,
    hub_recv,
    direct_send,
    direct_recv,
    relay_send,
    relay_recv,
    edge_send,
    edge_recv,
):
    months, firms, width = features.shape
    banks, sectors = bank_table.shape[0], sector_table.shape[0]
    slot = hub.shape[1]
    me, group = lax.axis_index("firm"), lax.axis_index("tm")
    even = lax.rem(me, 2) == 0
    partner = jnp.where(even, me + 1, me - 1)
    target = jnp.where(even, me + 2, me - 2)
    source = jnp.where(even, me - 2, me + 2)
    sends_on = jnp.logical_and(target >= 0, target < owners)
    gets_on = jnp.logical_and(source >= 0, source < owners)
    k_direct = jnp.where(even, 2, 0)
    k_relay = 2 - k_direct
    has_before, has_after = group > 0, group < groups - 1

    def month_at(step):
        return lax.rem(step + months - LAGS, months)

    def counts_copy(m):
        return pltpu.make_async_copy(counts_hbm.at[m], counts.at[m], counts_sem.at[m])

    def direct_copy(m):
        return pltpu.make_async_remote_copy(
            src_ref=supplied.at[m],
            dst_ref=direct.at[m],
            send_sem=direct_send.at[m],
            recv_sem=direct_recv.at[m],
            device_id={"firm": partner},
            device_id_type=MESH,
        )

    def relay_copy(m):
        return pltpu.make_async_remote_copy(
            src_ref=direct.at[m],
            dst_ref=relay.at[m],
            send_sem=relay_send.at[m],
            recv_sem=relay_recv.at[m],
            device_id={"firm": target},
            device_id_type=MESH,
        )

    def edge_copy(e):
        return pltpu.make_async_remote_copy(
            src_ref=normed_out.at[e],
            dst_ref=normed_in.at[e],
            send_sem=edge_send.at[e],
            recv_sem=edge_recv.at[e],
            device_id={"tm": group + 1},
            device_id_type=MESH,
        )

    def hub_copy(shift, owner):
        return pltpu.make_async_remote_copy(
            src_ref=hub.at[owner],
            dst_ref=hub.at[owner],
            send_sem=hub_send.at[shift],
            recv_sem=hub_recv.at[owner],
            device_id={"firm": lax.rem(me + shift, owners)},
            device_id_type=MESH,
        )

    barrier = pltpu.get_barrier_semaphore()

    @pl.loop(1, owners)
    def _(shift):
        pl.semaphore_signal(
            barrier, inc=1, device_id={"firm": lax.rem(me + shift, owners)}, device_id_type=MESH
        )

    @pl.when(has_before)
    def _():
        pl.semaphore_signal(barrier, inc=1, device_id={"tm": group - 1}, device_id_type=MESH)

    @pl.when(has_after)
    def _():
        pl.semaphore_signal(barrier, inc=1, device_id={"tm": group + 1}, device_id_type=MESH)

    @pl.loop(0, months)
    def _(step):
        counts_copy(month_at(step)).start()

    @pl.loop(0, months)
    def _(step):
        m = month_at(step)
        supplied[m] = dot(features[m], w_supply[...]).astype(BF16)

    hub_own[...] = jnp.zeros_like(hub_own)
    hub_own[0:banks] = bank_table[...].astype(F32)
    hub_own[banks : banks + sectors] = sector_table[...].astype(F32)
    hub[me] = hub_own[...].astype(BF16)

    row = lax.broadcasted_iota(jnp.int32, (width, width), 0)
    column = lax.broadcasted_iota(jnp.int32, (width, width), 1)
    size = width // HEADS
    same = row // size == column // size
    head_sum[...] = jnp.where(same, 0.5 / math.sqrt(size), 0.0).astype(BF16)

    @pl.when(jnp.logical_not(gets_on))
    def _():
        relay[...] = jnp.zeros_like(relay)

    @pl.when(jnp.logical_not(has_before))
    def _():
        normed_in[...] = jnp.zeros_like(normed_in)

    pl.semaphore_wait(
        barrier, owners - 1 + has_before.astype(jnp.int32) + has_after.astype(jnp.int32)
    )

    @pl.loop(1, owners)
    def _(shift):
        hub_copy(shift, me).start()

    @pl.loop(0, AHEAD)
    def _(step):
        direct_copy(month_at(step)).start()

    def pass_on(step):
        m = month_at(step)
        direct_copy(m).wait_recv()

        @pl.when(sends_on)
        def _():
            relay_copy(m).start()

        @pl.when(step + AHEAD < months)
        def _():
            direct_copy(month_at(step + AHEAD)).start()

    hub_rows = owners * slot
    hub_row = lax.broadcasted_iota(jnp.int32, (hub_rows, firms), 0)
    place = hub_row % slot
    bank_code = jnp.where(place < banks, hub_row // slot * banks + place, -1)
    sector_code = jnp.where(
        jnp.logical_and(place >= banks, place < banks + sectors),
        hub_row // slot * sectors + place - banks,
        -1,
    )

    def mix(step):
        m = month_at(step)
        counts_copy(m).wait()

        @pl.when(gets_on)
        def _():
            relay_copy(m).wait_recv()

        own = counts[m, 1].astype(F32)
        near = counts[m, k_direct].astype(F32)
        far = counts[m, k_relay].astype(F32)
        degree = 1.0 + jnp.sum(own + near + far, axis=-1, keepdims=True)
        message = dot(own.astype(BF16), supplied[m])
        message += dot(near.astype(BF16), direct[m])
        message += dot(far.astype(BF16), relay[m])
        chosen = jnp.logical_or(
            bank_code == bank_ids[pl.ds(m, 1), :], sector_code == sector_ids[pl.ds(m, 1), :]
        )
        hubs = lax.dot_general(
            jnp.where(chosen, 1.0, 0.0).astype(BF16),
            hub[...].reshape(hub_rows, width),
            (((0,), (0,)), ((), ())),
            preferred_element_type=F32,
        )
        total = features[m].astype(F32) + message * lax.rsqrt(degree) + hubs
        mixed[m] = total
        normed = rms_norm(total, gain_mix[...]).astype(BF16)
        query[m] = dot(normed, w_query[...]).astype(BF16)
        key[m + LAGS] = dot(normed, w_key[...]).astype(BF16)
        value[m + LAGS] = dot(normed, w_value[...]).astype(BF16)
        return normed

    def finish(m):
        q = query[m]
        total = jnp.zeros((firms, width), F32)
        for lag in range(LAGS + 1):
            score = dot(q * key[m + LAGS - lag], head_sum[...]) - 0.5 * math.log(4.0)
            total += (jnp.tanh(score) + 1.0) * value[m + LAGS - lag].astype(F32)
        second = mixed[m] + dot((0.5 * total).astype(BF16), w_out[...])
        normed = rms_norm(second, gain_ffn[...]).astype(BF16)
        hidden = w_in.shape[1]
        for part in range(0, hidden, width):
            x = dot(normed, w_in[:, part : part + width])
            inner = 0.5 * x * (1.0 + jnp.tanh(math.sqrt(2.0 / math.pi) * (x + 0.044715 * x * x * x)))
            second += dot(inner.astype(BF16), w_down[part : part + width, :])
        result[m] = second.astype(BF16)

    pass_on(0)

    @pl.loop(1, owners)
    def _(shift):
        hub_copy(shift, lax.rem(me + shift, owners)).wait_recv()

    @pl.loop(0, LAGS)
    def _(step):
        pass_on(step + 1)
        normed_out[step] = mix(step)

        @pl.when(has_after)
        def _():
            edge_copy(step).start()

    @pl.loop(0, LAGS)
    def _(e):
        @pl.when(has_before)
        def _():
            edge_copy(e).wait_recv()

        key[e] = dot(normed_in[e], w_key[...]).astype(BF16)
        value[e] = dot(normed_in[e], w_value[...]).astype(BF16)

    @pl.loop(LAGS, months - 1)
    def _(step):
        pass_on(step + 1)
        mix(step)
        finish(step - LAGS)

    mix(months - 1)

    @pl.loop(months - 1 - LAGS, months)
    def _(m):
        finish(m)

    @pl.loop(1, owners)
    def _(shift):
        hub_copy(shift, me).wait_send()

    @pl.loop(0, months)
    def _(m):
        direct_copy(m).wait_send()

        @pl.when(sends_on)
        def _():
            relay_copy(m).wait_send()

    @pl.when(has_after)
    def _():
        @pl.loop(0, LAGS)
        def _(e):
            edge_copy(e).wait_send()


def body(groups, owners, features, supply_counts, bank_ids, sector_ids, bank_table, sector_table, *rest):
    *weights, gain_mix, gain_ffn = rest
    months, firms, width = features.shape
    slot = -(-(bank_table.shape[0] + sector_table.shape[0]) // 16) * 16
    block = (months, firms, width)
    halo = (LAGS, firms, width)
    vmem = pl.BlockSpec(memory_space=pltpu.VMEM)
    dma = pltpu.SemaphoreType.DMA
    rows = months * firms
    return pl.pallas_call(
        functools.partial(kernel, groups, owners),
        out_shape=jax.ShapeDtypeStruct(block, BF16),
        in_specs=[vmem, pl.BlockSpec(memory_space=pl.ANY)] + [vmem] * 13,
        out_specs=vmem,
        scratch_shapes=[
            pltpu.VMEM((months, 3, firms, firms), jnp.int32),
            pltpu.VMEM((slot, width), F32),
            pltpu.VMEM((owners, slot, width), BF16),
            pltpu.VMEM(block, BF16),
            pltpu.VMEM(block, BF16),
            pltpu.VMEM(block, BF16),
            pltpu.VMEM(halo, BF16),
            pltpu.VMEM(halo, BF16),
            pltpu.VMEM(block, BF16),
            pltpu.VMEM((months + LAGS, firms, width), BF16),
            pltpu.VMEM((months + LAGS, firms, width), BF16),
            pltpu.VMEM(block, F32),
            pltpu.VMEM((width, width), BF16),
            dma((months,)),
            dma((owners,)),
            dma((owners,)),
            dma((months,)),
            dma((months,)),
            dma((months,)),
            dma((months,)),
            dma((LAGS,)),
            dma((LAGS,)),
        ],
        compiler_params=pltpu.CompilerParams(
            collective_id=0, has_side_effects=True, vmem_limit_bytes=56 * 1024 * 1024
        ),
        cost_estimate=pl.CostEstimate(
            flops=2 * rows * width * (width * 5 + 3 * firms + 8 * width),
            bytes_accessed=rows * (3 * firms * 4 + 4 * width),
            transcendentals=rows * width * 8,
        ),
    )(
        features,
        jnp.transpose(supply_counts, (0, 2, 1, 3)),
        bank_ids,
        sector_ids,
        bank_table,
        sector_table,
        *weights,
        gain_mix.reshape(1, width),
        gain_ffn.reshape(1, width),
    )


def solution(mesh):
    in_specs = (
        P("tm", "firm", None),
        P("tm", "firm", None, None),
        P("tm", "firm"),
        P("tm", "firm"),
        P("firm", None),
        P("firm", None),
    ) + (P(),) * 9
    return jax.shard_map(
        functools.partial(body, mesh.shape["tm"], mesh.shape["firm"]),
        mesh=mesh,
        in_specs=in_specs,
        out_specs=P("tm", "firm", None),
        check_vma=False,
    )
```

time: 172 us -> 46.7 us (0.27)
  the two profiles are of different devices: /device:TPU:0 before, /device:TPU:4 now
where the time goes in v1:
time: 46.7 us; the launch traced here: 46.4 us
  Pallas kernels  44.1 us (94%)
  local copies, waits for them, and re-layouts  2.26 us (5%)
    pallas_call x1, Pallas kernels, body(): pl.pallas_call(functools.partial(kernel, groups, owners), out_shape=jax.S...  44.1 us
    unnamed x1, local copies, waits for them, and re-layouts  2.26 us

profile of v1, /device:TPU:4, one launch (start us, length us, event | category | flops | bytes accessed | tf_op | source)
XLA Modules:
  0.0 46.4 jit_solution(6617577233342345378)
XLA Ops:
  0.0 44.1 %shard_map.145 = bf16[8,256,256]{2,1,0:T(8,128)(2,1)} custom-call(bf16[8,256,256]{2,1,0:T(8,128)(2,1)} %features.1, s32[8,3,256,256]{3,2,1,0:T(8,128)} %bitcast.3, s32[8,256]{1,0:T(8,128)} %bank_ids.1, s32[8,256]{1,0:T(8,128)} %sector_ids.1, bf16[8,256]{1,0:T(8,128)(2,1)} %bank_table.1, bf16[4,256]{1,0:T(4,128)(2,1)} %sector_table.1, ...), custom_call_target="tpu_custom_call" | custom-call | flops 4294967296 | bytes 8388608 | tf_op jit(solution)/shard_map/pallas_call | solution.py:319
  44.1 2.3 %copy.17 = bf16[8,256,256]{2,1,0:T(8,128)(2,1)} copy(bf16[8,256,256]{2,1,0:T(8,128)(2,1)} %shard_map.145) | data formatting | bytes 2097152

commit v2 on v1

--- a/solution.py
+++ b/solution.py
@@ -11,6 +11,7 @@
 HEADS = 4
 LAGS = 3
 AHEAD = 3
+HALVES = 2
 MESH = pl.DeviceIdType.MESH
 F32 = jnp.float32
 BF16 = jnp.bfloat16
@@ -28,12 +29,23 @@
 def kernel(
     groups,
     owners,
-    features,
+    features_hbm,
     counts_hbm,
     bank_ids,
     sector_ids,
     bank_table,
     sector_table,
+    w_supply_hbm,
+    w_query_hbm,
+    w_key_hbm,
+    w_value_hbm,
+    w_out_hbm,
+    w_in_hbm,
+    w_down_hbm,
+    gain_mix,
+    gain_ffn,
+    result_hbm,
+    features,
     w_supply,
     w_query,
     w_key,
@@ -41,8 +53,6 @@
     w_out,
     w_in,
     w_down,
-    gain_mix,
-    gain_ffn,
     result,
     counts,
     hub_own,
@@ -57,6 +67,8 @@
     value,
     mixed,
     head_sum,
+    load_sem,
+    result_sem,
     counts_sem,
     hub_send,
     hub_recv,
@@ -87,22 +99,42 @@
     def counts_copy(m):
         return pltpu.make_async_copy(counts_hbm.at[m], counts.at[m], counts_sem.at[m])
 
-    def direct_copy(m):
+    def result_copy(m):
+        return pltpu.make_async_copy(result.at[m], result_hbm.at[m], result_sem.at[m])
+
+    loads = [
+        pltpu.make_async_copy(src, dst, load_sem.at[i])
+        for i, (src, dst) in enumerate(
+            [
+                (w_supply_hbm, w_supply),
+                (features_hbm, features),
+                (w_query_hbm, w_query),
+                (w_key_hbm, w_key),
+                (w_value_hbm, w_value),
+                (w_out_hbm, w_out),
+                (w_in_hbm, w_in),
+                (w_down_hbm, w_down),
+            ]
+        )
+    ]
+    half = firms // HALVES
+
+    def direct_copy(m, h):
         return pltpu.make_async_remote_copy(
-            src_ref=supplied.at[m],
-            dst_ref=direct.at[m],
-            send_sem=direct_send.at[m],
-            recv_sem=direct_recv.at[m],
+            src_ref=supplied.at[m, pl.ds(h * half, half)],
+            dst_ref=direct.at[m, pl.ds(h * half, half)],
+            send_sem=direct_send.at[m * HALVES + h],
+            recv_sem=direct_recv.at[m * HALVES + h],
             device_id={"firm": partner},
             device_id_type=MESH,
         )
 
-    def relay_copy(m):
+    def relay_copy(m, h):
         return pltpu.make_async_remote_copy(
-            src_ref=direct.at[m],
-            dst_ref=relay.at[m],
-            send_sem=relay_send.at[m],
-            recv_sem=relay_recv.at[m],
+            src_ref=direct.at[m, pl.ds(h * half, half)],
+            dst_ref=relay.at[m, pl.ds(h * half, half)],
+            send_sem=relay_send.at[m * HALVES + h],
+            recv_sem=relay_recv.at[m * HALVES + h],
             device_id={"firm": target},
             device_id_type=MESH,
         )
@@ -143,14 +175,15 @@
     def _():
         pl.semaphore_signal(barrier, inc=1, device_id={"tm": group + 1}, device_id_type=MESH)
 
+    for load in loads[:2]:
+        load.start()
+
     @pl.loop(0, months)
     def _(step):
         counts_copy(month_at(step)).start()
 
-    @pl.loop(0, months)
-    def _(step):
-        m = month_at(step)
-        supplied[m] = dot(features[m], w_supply[...]).astype(BF16)
+    for load in loads[2:]:
+        load.start()
 
     hub_own[...] = jnp.zeros_like(hub_own)
     hub_own[0:banks] = bank_table[...].astype(F32)
@@ -163,6 +196,14 @@
     same = row // size == column // size
     head_sum[...] = jnp.where(same, 0.5 / math.sqrt(size), 0.0).astype(BF16)
 
+    for load in loads[:2]:
+        load.wait()
+    for low, high in ((months - LAGS, months), (0, months - LAGS)):
+        rows = features[low:high].reshape((high - low) * firms, width)
+        supplied[low:high] = (
+            dot(rows, w_supply[...]).astype(BF16).reshape(high - low, firms, width)
+        )
+
     @pl.when(jnp.logical_not(gets_on))
     def _():
         relay[...] = jnp.zeros_like(relay)
@@ -181,19 +222,26 @@
 
     @pl.loop(0, AHEAD)
     def _(step):
-        direct_copy(month_at(step)).start()
+        for h in range(HALVES):
+            direct_copy(month_at(step), h).start()
+
+    for load in loads[2:]:
+        load.wait()
 
     def pass_on(step):
         m = month_at(step)
-        direct_copy(m).wait_recv()
-
-        @pl.when(sends_on)
-        def _():
-            relay_copy(m).start()
 
         @pl.when(step + AHEAD < months)
         def _():
-            direct_copy(month_at(step + AHEAD)).start()
+            for h in range(HALVES):
+                direct_copy(month_at(step + AHEAD), h).start()
+
+        for h in range(HALVES):
+            direct_copy(m, h).wait_recv()
+
+            @pl.when(sends_on)
+            def _():
+                relay_copy(m, h).start()
 
     hub_rows = owners * slot
     hub_row = lax.broadcasted_iota(jnp.int32, (hub_rows, firms), 0)
@@ -208,18 +256,12 @@
     def mix(step):
         m = month_at(step)
         counts_copy(m).wait()
-
-        @pl.when(gets_on)
-        def _():
-            relay_copy(m).wait_recv()
-
         own = counts[m, 1].astype(F32)
         near = counts[m, k_direct].astype(F32)
         far = counts[m, k_relay].astype(F32)
-        degree = 1.0 + jnp.sum(own + near + far, axis=-1, keepdims=True)
+        scale = lax.rsqrt(1.0 + jnp.sum(own + near + far, axis=-1, keepdims=True))
         message = dot(own.astype(BF16), supplied[m])
         message += dot(near.astype(BF16), direct[m])
-        message += dot(far.astype(BF16), relay[m])
         chosen = jnp.logical_or(
             bank_code == bank_ids[pl.ds(m, 1), :], sector_code == sector_ids[pl.ds(m, 1), :]
         )
@@ -229,7 +271,14 @@
             (((0,), (0,)), ((), ())),
             preferred_element_type=F32,
         )
-        total = features[m].astype(F32) + message * lax.rsqrt(degree) + hubs
+        mixed[m] = features[m].astype(F32) + message * scale + hubs
+
+        @pl.when(gets_on)
+        def _():
+            for h in range(HALVES):
+                relay_copy(m, h).wait_recv()
+
+        total = mixed[m] + dot(counts[m, k_relay].astype(F32).astype(BF16), relay[m]) * scale
         mixed[m] = total
         normed = rms_norm(total, gain_mix[...]).astype(BF16)
         query[m] = dot(normed, w_query[...]).astype(BF16)
@@ -237,20 +286,29 @@
         value[m + LAGS] = dot(normed, w_value[...]).astype(BF16)
         return normed
 
-    def finish(m):
-        q = query[m]
-        total = jnp.zeros((firms, width), F32)
+    def finish(first, span):
+        rows = span * firms
+
+        def block(ref, start):
+            return ref[pl.ds(start, span)].reshape(rows, width)
+
+        q = block(query, first)
+        pairs = [q * block(key, first + LAGS - lag) for lag in range(LAGS + 1)]
+        scores = dot(jnp.concatenate(pairs, axis=0), head_sum[...]) - 0.5 * math.log(4.0)
+        total = jnp.zeros((rows, width), F32)
         for lag in range(LAGS + 1):
-            score = dot(q * key[m + LAGS - lag], head_sum[...]) - 0.5 * math.log(4.0)
-            total += (jnp.tanh(score) + 1.0) * value[m + LAGS - lag].astype(F32)
-        second = mixed[m] + dot((0.5 * total).astype(BF16), w_out[...])
+            weight = jnp.tanh(scores[lag * rows : (lag + 1) * rows]) + 1.0
+            total += weight * block(value, first + LAGS - lag).astype(F32)
+        second = block(mixed, first) + dot((0.5 * total).astype(BF16), w_out[...])
         normed = rms_norm(second, gain_ffn[...]).astype(BF16)
         hidden = w_in.shape[1]
         for part in range(0, hidden, width):
             x = dot(normed, w_in[:, part : part + width])
             inner = 0.5 * x * (1.0 + jnp.tanh(math.sqrt(2.0 / math.pi) * (x + 0.044715 * x * x * x)))
             second += dot(inner.astype(BF16), w_down[part : part + width, :])
-        result[m] = second.astype(BF16)
+        result[pl.ds(first, span)] = second.astype(BF16).reshape(span, firms, width)
+        for i in range(span):
+            result_copy(first + i).start()
 
     pass_on(0)
 
@@ -280,13 +338,11 @@
     def _(step):
         pass_on(step + 1)
         mix(step)
-        finish(step - LAGS)
+        finish(step - LAGS, 1)
 
     mix(months - 1)
 
-    @pl.loop(months - 1 - LAGS, months)
-    def _(m):
-        finish(m)
+    finish(months - 1 - LAGS, LAGS + 1)
 
     @pl.loop(1, owners)
     def _(shift):
@@ -294,17 +350,32 @@
 
     @pl.loop(0, months)
     def _(m):
-        direct_copy(m).wait_send()
+        for h in range(HALVES):
+            direct_copy(m, h).wait_send()
 
         @pl.when(sends_on)
         def _():
-            relay_copy(m).wait_send()
+            for h in range(HALVES):
+                relay_copy(m, h).wait_send()
+
+        result_copy(m).wait()
 
     @pl.when(has_after)
     def _():
         @pl.loop(0, LAGS)
         def _(e):
             edge_copy(e).wait_send()
+
+
+def copy_kernel(source, result, sem):
+    copies = [
+        pltpu.make_async_copy(source.at[m], result.at[m], sem.at[m])
+        for m in range(source.shape[0])
+    ]
+    for copy in copies:
+        copy.start()
+    for copy in copies:
+        copy.wait()
 
 
 def body(groups, owners, features, supply_counts, bank_ids, sector_ids, bank_table, sector_table, *rest):
@@ -316,12 +387,24 @@
     vmem = pl.BlockSpec(memory_space=pltpu.VMEM)
     dma = pltpu.SemaphoreType.DMA
     rows = months * firms
-    return pl.pallas_call(
+    hbm = pl.BlockSpec(memory_space=pl.ANY)
+    hidden = weights[-1].shape[0]
+    square = pltpu.VMEM((width, width), BF16)
+    out = pl.pallas_call(
         functools.partial(kernel, groups, owners),
         out_shape=jax.ShapeDtypeStruct(block, BF16),
-        in_specs=[vmem, pl.BlockSpec(memory_space=pl.ANY)] + [vmem] * 13,
-        out_specs=vmem,
+        in_specs=[hbm] * 2 + [vmem] * 4 + [hbm] * 7 + [vmem] * 2,
+        out_specs=hbm,
         scratch_shapes=[
+            pltpu.VMEM(block, BF16),
+            square,
+            square,
+            square,
+            square,
+            square,
+            pltpu.VMEM((width, hidden), BF16),
+            pltpu.VMEM((hidden, width), BF16),
+            pltpu.VMEM(block, BF16),
             pltpu.VMEM((months, 3, firms, firms), jnp.int32),
             pltpu.VMEM((slot, width), F32),
             pltpu.VMEM((owners, slot, width), BF16),
@@ -335,13 +418,15 @@
             pltpu.VMEM((months + LAGS, firms, width), BF16),
             pltpu.VMEM(block, F32),
             pltpu.VMEM((width, width), BF16),
+            dma((8,)),
+            dma((months,)),
             dma((months,)),
             dma((owners,)),
             dma((owners,)),
-            dma((months,)),
-            dma((months,)),
-            dma((months,)),
-            dma((months,)),
+            dma((HALVES * months,)),
+            dma((HALVES * months,)),
+            dma((HALVES * months,)),
+            dma((HALVES * months,)),
             dma((LAGS,)),
             dma((LAGS,)),
         ],
@@ -364,6 +449,14 @@
         gain_mix.reshape(1, width),
         gain_ffn.reshape(1, width),
     )
+    return pl.pallas_call(
+        copy_kernel,
+        out_shape=jax.ShapeDtypeStruct(block, BF16),
+        in_specs=[pl.BlockSpec(memory_space=pltpu.HBM)],
+        out_specs=pl.BlockSpec(memory_space=pltpu.HBM),
+        scratch_shapes=[dma((months,))],
+        compiler_params=pltpu.CompilerParams(vmem_limit_bytes=56 * 1024 * 1024),
+    )(out)
 
 
 def solution(mesh):

time: 46.7 us -> 73.3 us (1.57)
  Pallas kernels: 44.1 us -> 73.1 us
  local copies, waits for them, and re-layouts: 2.26 us -> 0 us
    pallas_call x0 -> x1, Pallas kernels: none -> 32.9 us  [body(): pl.pallas_call(copy_kernel, out_shape=jax.ShapeDtypeStruct(block, BF16),...]
    pallas_call x1, Pallas kernels: 44.1 us -> 40.2 us  [body(): pl.pallas_call(functools.partial(kernel, groups, owners), out_shape=jax.S...]
    unnamed x1 -> x0, local copies, waits for them, and re-layouts: 2.26 us -> none
where the time goes in v2:
time: 73.3 us; the launch traced here: 73.1 us
  Pallas kernels  73.1 us (100%)
    pallas_call x1, Pallas kernels, body(): pl.pallas_call(functools.partial(kernel, groups, owners), out_shape=jax.S...  40.2 us
    pallas_call x1, Pallas kernels, body(): pl.pallas_call(copy_kernel, out_shape=jax.ShapeDtypeStruct(block, BF16),...  32.9 us

profile of v2, /device:TPU:4, one launch (start us, length us, event | category | flops | bytes accessed | tf_op | source)
XLA Modules:
  0.0 73.1 jit_solution(7151606411110218829)
XLA Ops:
  0.0 40.2 %shard_map.145.source = bf16[8,256,256]{2,1,0:T(8,128)(2,1)} custom-call(bf16[8,256,256]{2,1,0:T(8,128)(2,1)} %features_hbm.1, s32[8,3,256,256]{3,2,1,0:T(8,128)} %bitcast.3, s32[8,256]{1,0:T(8,128)} %bank_ids.1, s32[8,256]{1,0:T(8,128)} %sector_ids.1, bf16[8,256]{1,0:T(8,128)(2,1)} %bank_table.1, bf16[4,256]{1,0:T(4,128)(2,1)} %sector_table.1, ...), custom_call_target="tpu_custom_call" | custom-call | flops 4294967296 | bytes 8388608 | tf_op jit(solution)/shard_map/pallas_call | solution.py:393
  40.2 32.9 %shard_map.146 = bf16[8,256,256]{2,1,0:T(8,128)(2,1)} custom-call(bf16[8,256,256]{2,1,0:T(8,128)(2,1)} %shard_map.145.source), custom_call_target="tpu_custom_call" | custom-call | tf_op jit(solution)/shard_map/pallas_call | solution.py:452

commit v3 on v2

--- a/solution.py
+++ b/solution.py
@@ -12,6 +12,7 @@
 LAGS = 3
 AHEAD = 3
 HALVES = 2
+CURVE = math.sqrt(2.0 / math.pi)
 MESH = pl.DeviceIdType.MESH
 F32 = jnp.float32
 BF16 = jnp.bfloat16
@@ -44,7 +45,7 @@
     w_down_hbm,
     gain_mix,
     gain_ffn,
-    result_hbm,
+    result,
     features,
     w_supply,
     w_query,
@@ -53,7 +54,6 @@
     w_out,
     w_in,
     w_down,
-    result,
     counts,
     hub_own,
     hub,
@@ -68,7 +68,6 @@
     mixed,
     head_sum,
     load_sem,
-    result_sem,
     counts_sem,
     hub_send,
     hub_recv,
@@ -99,15 +98,13 @@
     def counts_copy(m):
         return pltpu.make_async_copy(counts_hbm.at[m], counts.at[m], counts_sem.at[m])
 
-    def result_copy(m):
-        return pltpu.make_async_copy(result.at[m], result_hbm.at[m], result_sem.at[m])
-
     loads = [
         pltpu.make_async_copy(src, dst, load_sem.at[i])
         for i, (src, dst) in enumerate(
             [
                 (w_supply_hbm, w_supply),
-                (features_hbm, features),
+                (features_hbm.at[months - LAGS : months], features.at[months - LAGS : months]),
+                (features_hbm.at[0 : months - LAGS], features.at[0 : months - LAGS]),
                 (w_query_hbm, w_query),
                 (w_key_hbm, w_key),
                 (w_value_hbm, w_value),
@@ -175,20 +172,45 @@
     def _():
         pl.semaphore_signal(barrier, inc=1, device_id={"tm": group + 1}, device_id_type=MESH)
 
-    for load in loads[:2]:
+    for load in loads[:3]:
         load.start()
 
     @pl.loop(0, months)
     def _(step):
         counts_copy(month_at(step)).start()
 
-    for load in loads[2:]:
+    for load in loads[3:]:
         load.start()
+
+    def supply(low, high):
+        rows = features[low:high].reshape((high - low) * firms, width)
+        supplied[low:high] = (
+            dot(rows, w_supply[...]).astype(BF16).reshape(high - low, firms, width)
+        )
+
+    for load in loads[:2]:
+        load.wait()
+    supply(months - LAGS, months)
+    pl.semaphore_wait(
+        barrier, owners - 1 + has_before.astype(jnp.int32) + has_after.astype(jnp.int32)
+    )
+
+    @pl.loop(0, AHEAD)
+    def _(step):
+        for h in range(HALVES):
+            direct_copy(month_at(step), h).start()
 
     hub_own[...] = jnp.zeros_like(hub_own)
     hub_own[0:banks] = bank_table[...].astype(F32)
     hub_own[banks : banks + sectors] = sector_table[...].astype(F32)
     hub[me] = hub_own[...].astype(BF16)
+
+    @pl.loop(1, owners)
+    def _(shift):
+        hub_copy(shift, me).start()
+
+    loads[2].wait()
+    supply(0, months - LAGS)
 
     row = lax.broadcasted_iota(jnp.int32, (width, width), 0)
     column = lax.broadcasted_iota(jnp.int32, (width, width), 1)
@@ -196,14 +218,6 @@
     same = row // size == column // size
     head_sum[...] = jnp.where(same, 0.5 / math.sqrt(size), 0.0).astype(BF16)
 
-    for load in loads[:2]:
-        load.wait()
-    for low, high in ((months - LAGS, months), (0, months - LAGS)):
-        rows = features[low:high].reshape((high - low) * firms, width)
-        supplied[low:high] = (
-            dot(rows, w_supply[...]).astype(BF16).reshape(high - low, firms, width)
-        )
-
     @pl.when(jnp.logical_not(gets_on))
     def _():
         relay[...] = jnp.zeros_like(relay)
@@ -212,21 +226,9 @@
     def _():
         normed_in[...] = jnp.zeros_like(normed_in)
 
-    pl.semaphore_wait(
-        barrier, owners - 1 + has_before.astype(jnp.int32) + has_after.astype(jnp.int32)
-    )
-
-    @pl.loop(1, owners)
-    def _(shift):
-        hub_copy(shift, me).start()
-
-    @pl.loop(0, AHEAD)
-    def _(step):
-        for h in range(HALVES):
-            direct_copy(month_at(step), h).start()
-
-    for load in loads[2:]:
+    for load in loads[3:]:
         load.wait()
+    w_down[...] = w_down[...] * 0.5
 
     def pass_on(step):
         m = month_at(step)
@@ -304,11 +306,9 @@
         hidden = w_in.shape[1]
         for part in range(0, hidden, width):
             x = dot(normed, w_in[:, part : part + width])
-            inner = 0.5 * x * (1.0 + jnp.tanh(math.sqrt(2.0 / math.pi) * (x + 0.044715 * x * x * x)))
+            inner = x + x * jnp.tanh(x * (CURVE + 0.044715 * CURVE * (x * x)))
             second += dot(inner.astype(BF16), w_down[part : part + width, :])
         result[pl.ds(first, span)] = second.astype(BF16).reshape(span, firms, width)
-        for i in range(span):
-            result_copy(first + i).start()
 
     pass_on(0)
 
@@ -357,8 +357,6 @@
         def _():
             for h in range(HALVES):
                 relay_copy(m, h).wait_send()
-
-        result_copy(m).wait()
 
     @pl.when(has_after)
     def _():
@@ -387,14 +385,14 @@
     vmem = pl.BlockSpec(memory_space=pltpu.VMEM)
     dma = pltpu.SemaphoreType.DMA
     rows = months * firms
-    hbm = pl.BlockSpec(memory_space=pl.ANY)
+    hbm = pl.BlockSpec(memory_space=pltpu.HBM)
     hidden = weights[-1].shape[0]
     square = pltpu.VMEM((width, width), BF16)
     out = pl.pallas_call(
         functools.partial(kernel, groups, owners),
         out_shape=jax.ShapeDtypeStruct(block, BF16),
         in_specs=[hbm] * 2 + [vmem] * 4 + [hbm] * 7 + [vmem] * 2,
-        out_specs=hbm,
+        out_specs=vmem,
         scratch_shapes=[
             pltpu.VMEM(block, BF16),
             square,
@@ -404,7 +402,6 @@
             square,
             pltpu.VMEM((width, hidden), BF16),
             pltpu.VMEM((hidden, width), BF16),
-            pltpu.VMEM(block, BF16),
             pltpu.VMEM((months, 3, firms, firms), jnp.int32),
             pltpu.VMEM((slot, width), F32),
             pltpu.VMEM((owners, slot, width), BF16),
@@ -418,8 +415,7 @@
             pltpu.VMEM((months + LAGS, firms, width), BF16),
             pltpu.VMEM(block, F32),
             pltpu.VMEM((width, width), BF16),
-            dma((8,)),
-            dma((months,)),
+            dma((9,)),
             dma((months,)),
             dma((owners,)),
             dma((owners,)),
@@ -431,7 +427,7 @@
             dma((LAGS,)),
         ],
         compiler_params=pltpu.CompilerParams(
-            collective_id=0, has_side_effects=True, vmem_limit_bytes=56 * 1024 * 1024
+            collective_id=0, has_side_effects=True, vmem_limit_bytes=50 * 1024 * 1024
         ),
         cost_estimate=pl.CostEstimate(
             flops=2 * rows * width * (width * 5 + 3 * firms + 8 * width),
@@ -452,10 +448,9 @@
     return pl.pallas_call(
         copy_kernel,
         out_shape=jax.ShapeDtypeStruct(block, BF16),
-        in_specs=[pl.BlockSpec(memory_space=pltpu.HBM)],
-        out_specs=pl.BlockSpec(memory_space=pltpu.HBM),
+        in_specs=[vmem],
+        out_specs=hbm,
         scratch_shapes=[dma((months,))],
-        compiler_params=pltpu.CompilerParams(vmem_limit_bytes=56 * 1024 * 1024),
     )(out)
 
 

time: 73.3 us -> 58.8 us (0.80)
  Pallas kernels: 73.1 us -> 45.3 us
  local copies, waits for them, and re-layouts: 0 us -> 12.9 us
    pallas_call x1, Pallas kernels: 32.9 us -> 2.25 us  [body(): pl.pallas_call(copy_kernel, out_shape=jax.ShapeDtypeStruct(block, BF16),...]
    unnamed x0 -> x30, local copies, waits for them, and re-layouts: none -> 12.9 us
    pallas_call x1, Pallas kernels: 40.2 us -> 43.1 us  [body(): pl.pallas_call(functools.partial(kernel, groups, owners), out_shape=jax.S...]
where the time goes in v3:
time: 58.8 us; the launch traced here: 58.3 us
  Pallas kernels  45.3 us (77%)
  local copies, waits for them, and re-layouts  12.9 us (22%)
    pallas_call x1, Pallas kernels, body(): pl.pallas_call(functools.partial(kernel, groups, owners), out_shape=jax.S...  43.1 us
    unnamed x30, local copies, waits for them, and re-layouts  12.9 us
    pallas_call x1, Pallas kernels, body(): pl.pallas_call(copy_kernel, out_shape=jax.ShapeDtypeStruct(block, BF16),...  2.25 us

profile of v3, /device:TPU:4, one launch (start us, length us, event | category | flops | bytes accessed | tf_op | source)
XLA Modules:
  0.0 58.3 jit_solution(7651912632378392057)
XLA Ops:
  0.0 0.0 copy-start.1
  0.0 1.2 %copy-done.1 = bf16[8,256,256]{2,1,0:T(8,128)(2,1)S(1)} copy-done((bf16[8,256,256]{2,1,0:T(8,128)(2,1)S(1)}, bf16[8,256,256]{2,1,0:T(8,128)(2,1)}, u32[]{:S(2)}) %copy-start.1) | copy-done | bytes 1048600
  1.2 0.0 copy-start.2
  1.2 1.0 %copy-done.2 = bf16[256,1024]{1,0:T(8,128)(2,1)S(1)} copy-done((bf16[256,1024]{1,0:T(8,128)(2,1)S(1)}, bf16[256,1024]{1,0:T(8,128)(2,1)}, u32[]{:S(2)}) %copy-start.2) | copy-done | bytes 524312
  2.3 0.0 copy-start.3
  2.3 1.0 %copy-done.3 = bf16[1024,256]{1,0:T(8,128)(2,1)S(1)} copy-done((bf16[1024,256]{1,0:T(8,128)(2,1)S(1)}, bf16[1024,256]{1,0:T(8,128)(2,1)}, u32[]{:S(2)}) %copy-start.3) | copy-done | bytes 524312
  3.3 0.0 copy-start.4
  3.3 0.9 %copy-done.4 = bf16[256,256]{1,0:T(8,128)(2,1)S(1)} copy-done((bf16[256,256]{1,0:T(8,128)(2,1)S(1)}, bf16[256,256]{1,0:T(8,128)(2,1)}, u32[]{:S(2)}) %copy-start.4) | copy-done | bytes 131096
  4.2 0.0 copy-start.5
  4.2 0.9 %copy-done.5 = bf16[256,256]{1,0:T(8,128)(2,1)S(1)} copy-done((bf16[256,256]{1,0:T(8,128)(2,1)S(1)}, bf16[256,256]{1,0:T(8,128)(2,1)}, u32[]{:S(2)}) %copy-start.5) | copy-done | bytes 131096
  5.1 0.0 copy-start.6
  5.1 0.9 %copy-done.6 = bf16[256,256]{1,0:T(8,128)(2,1)S(1)} copy-done((bf16[256,256]{1,0:T(8,128)(2,1)S(1)}, bf16[256,256]{1,0:T(8,128)(2,1)}, u32[]{:S(2)}) %copy-start.6) | copy-done | bytes 131096
  6.0 0.0 copy-start.7
  6.0 0.9 %copy-done.7 = bf16[256,256]{1,0:T(8,128)(2,1)S(1)} copy-done((bf16[256,256]{1,0:T(8,128)(2,1)S(1)}, bf16[256,256]{1,0:T(8,128)(2,1)}, u32[]{:S(2)}) %copy-start.7) | copy-done | bytes 131096
  6.9 0.0 copy-start.8
  6.9 0.9 %copy-done.8 = bf16[256,256]{1,0:T(8,128)(2,1)S(1)} copy-done((bf16[256,256]{1,0:T(8,128)(2,1)S(1)}, bf16[256,256]{1,0:T(8,128)(2,1)}, u32[]{:S(2)}) %copy-start.8) | copy-done | bytes 131096
  7.8 0.0 copy-start.9
  7.8 0.7 %copy-done.9 = s32[8,256]{1,0:T(8,128)S(1)} copy-done((s32[8,256]{1,0:T(8,128)S(1)}, s32[8,256]{1,0:T(8,128)}, u32[]{:S(2)}) %copy-start.9) | copy-done | bytes 8216
  8.5 0.0 copy-start.10
  8.5 0.7 %copy-done.10 = s32[8,256]{1,0:T(8,128)S(1)} copy-done((s32[8,256]{1,0:T(8,128)S(1)}, s32[8,256]{1,0:T(8,128)}, u32[]{:S(2)}) %copy-start.10) | copy-done | bytes 8216
  9.2 0.0 copy-start.11
  9.2 0.7 %copy-done.11 = bf16[8,256]{1,0:T(8,128)(2,1)S(1)} copy-done((bf16[8,256]{1,0:T(8,128)(2,1)S(1)}, bf16[8,256]{1,0:T(8,128)(2,1)}, u32[]{:S(2)}) %copy-start.11) | copy-done | bytes 4120
  9.9 0.0 copy-start.12
  9.9 0.7 %copy-done.12 = bf16[4,256]{1,0:T(4,128)(2,1)S(1)} copy-done((bf16[4,256]{1,0:T(4,128)(2,1)S(1)}, bf16[4,256]{1,0:T(4,128)(2,1)}, u32[]{:S(2)}) %copy-start.12) | copy-done | bytes 2072
  10.6 0.0 copy-start.13
  10.6 0.7 %copy-done.13 = f32[256]{0:T(256)S(1)} copy-done((f32[256]{0:T(256)S(1)}, f32[256]{0:T(256)}, u32[]{:S(2)}) %copy-start.13) | copy-done | bytes 1048
  11.3 0.0 copy-start.14
  11.3 0.7 %copy-done.14 = f32[256]{0:T(256)S(1)} copy-done((f32[256]{0:T(256)S(1)}, f32[256]{0:T(256)}, u32[]{:S(2)}) %copy-start.14) | copy-done | bytes 1048
  12.0 43.1 %shard_map.145.source = bf16[8,256,256]{2,1,0:T(8,128)(2,1)S(1)} custom-call(bf16[8,256,256]{2,1,0:T(8,128)(2,1)S(1)} %copy-done.1, s32[8,3,256,256]{3,2,1,0:T(8,128)} %bitcast.5, s32[8,256]{1,0:T(8,128)S(1)} %copy-done.9, s32[8,256]{1,0:T(8,128)S(1)} %copy-done.10, bf16[8,256]{1,0:T(8,128)(2,1)S(1)} %copy-done.11, bf16[4,256]{1,0:T(4,128)(2,1)S(1)} %copy-done.12, ...), custom_call_target="tpu_custom_call" | custom-call | flops 4294967296 | bytes 8388608 | tf_op jit(solution)/shard_map/pallas_call | solution.py:391
  55.1 0.0 copy-start
  55.1 1.0 %copy-done = bf16[8,256,256]{2,1,0:T(8,128)(2,1)} copy-done((bf16[8,256,256]{2,1,0:T(8,128)(2,1)}, bf16[8,256,256]{2,1,0:T(8,128)(2,1)S(1)}, u32[]{:S(2)}) %copy-start) | copy-done | bytes 1048600
  56.0 2.2 %shard_map.146 = bf16[8,256,256]{2,1,0:T(8,128)(2,1)} custom-call(bf16[8,256,256]{2,1,0:T(8,128)(2,1)} %copy-done), custom_call_target="tpu_custom_call" | custom-call | tf_op jit(solution)/shard_map/pallas_call | solution.py:448
Async XLA Ops:
  0.0 1.2 %copy-start.1 = (bf16[8,256,256]{2,1,0:T(8,128)(2,1)S(1)}, bf16[8,256,256]{2,1,0:T(8,128)(2,1)}, u32[]{:S(2)}) copy-start(bf16[8,256,256]{2,1,0:T(8,128)(2,1)} %features_hbm.1) | copy-start | bytes 3145732
  1.2 1.0 %copy-start.2 = (bf16[256,1024]{1,0:T(8,128)(2,1)S(1)}, bf16[256,1024]{1,0:T(8,128)(2,1)}, u32[]{:S(2)}) copy-start(bf16[256,1024]{1,0:T(8,128)(2,1)} %w_in_hbm.1) | copy-start | bytes 1572868
  2.3 1.0 %copy-start.3 = (bf16[1024,256]{1,0:T(8,128)(2,1)S(1)}, bf16[1024,256]{1,0:T(8,128)(2,1)}, u32[]{:S(2)}) copy-start(bf16[1024,256]{1,0:T(8,128)(2,1)} %w_down_hbm.1) | copy-start | bytes 1572868
  3.3 0.9 %copy-start.4 = (bf16[256,256]{1,0:T(8,128)(2,1)S(1)}, bf16[256,256]{1,0:T(8,128)(2,1)}, u32[]{:S(2)}) copy-start(bf16[256,256]{1,0:T(8,128)(2,1)} %w_supply_hbm.1) | copy-start | bytes 393220
  4.2 0.9 %copy-start.5 = (bf16[256,256]{1,0:T(8,128)(2,1)S(1)}, bf16[256,256]{1,0:T(8,128)(2,1)}, u32[]{:S(2)}) copy-start(bf16[256,256]{1,0:T(8,128)(2,1)} %w_query_hbm.1) | copy-start | bytes 393220
  5.1 0.9 %copy-start.6 = (bf16[256,256]{1,0:T(8,128)(2,1)S(1)}, bf16[256,256]{1,0:T(8,128)(2,1)}, u32[]{:S(2)}) copy-start(bf16[256,256]{1,0:T(8,128)(2,1)} %w_key_hbm.1) | copy-start | bytes 393220
  6.0 0.9 %copy-start.7 = (bf16[256,256]{1,0:T(8,128)(2,1)S(1)}, bf16[256,256]{1,0:T(8,128)(2,1)}, u32[]{:S(2)}) copy-start(bf16[256,256]{1,0:T(8,128)(2,1)} %w_value_hbm.1) | copy-start | bytes 393220
  6.9 0.9 %copy-start.8 = (bf16[256,256]{1,0:T(8,128)(2,1)S(1)}, bf16[256,256]{1,0:T(8,128)(2,1)}, u32[]{:S(2)}) copy-start(bf16[256,256]{1,0:T(8,128)(2,1)} %w_out_hbm.1) | copy-start | bytes 393220
  7.8 0.7 %copy-start.9 = (s32[8,256]{1,0:T(8,128)S(1)}, s32[8,256]{1,0:T(8,128)}, u32[]{:S(2)}) copy-start(s32[8,256]{1,0:T(8,128)} %bank_ids.1) | copy-start | bytes 24580
  8.5 0.7 %copy-start.10 = (s32[8,256]{1,0:T(8,128)S(1)}, s32[8,256]{1,0:T(8,128)}, u32[]{:S(2)}) copy-start(s32[8,256]{1,0:T(8,128)} %sector_ids.1) | copy-start | bytes 24580
  9.2 0.7 %copy-start.11 = (bf16[8,256]{1,0:T(8,128)(2,1)S(1)}, bf16[8,256]{1,0:T(8,128)(2,1)}, u32[]{:S(2)}) copy-start(bf16[8,256]{1,0:T(8,128)(2,1)} %bank_table.1) | copy-start | bytes 12292
  9.9 0.7 %copy-start.12 = (bf16[4,256]{1,0:T(4,128)(2,1)S(1)}, bf16[4,256]{1,0:T(4,128)(2,1)}, u32[]{:S(2)}) copy-start(bf16[4,256]{1,0:T(4,128)(2,1)} %sector_table.1) | copy-start | bytes 6148
  10.6 0.7 %copy-start.13 = (f32[256]{0:T(256)S(1)}, f32[256]{0:T(256)}, u32[]{:S(2)}) copy-start(f32[256]{0:T(256)} %param.28) | copy-start | bytes 3076
  11.3 0.7 %copy-start.14 = (f32[256]{0:T(256)S(1)}, f32[256]{0:T(256)}, u32[]{:S(2)}) copy-start(f32[256]{0:T(256)} %param.29) | copy-start | bytes 3076
  55.1 1.0 %copy-start = (bf16[8,256,256]{2,1,0:T(8,128)(2,1)}, bf16[8,256,256]{2,1,0:T(8,128)(2,1)S(1)}, u32[]{:S(2)}) copy-start(bf16[8,256,256]{2,1,0:T(8,128)(2,1)S(1)} %shard_map.145.source) | copy-start | bytes 3145732

commit v4 on v3

--- a/solution.py
+++ b/solution.py
@@ -303,11 +303,12 @@
             total += weight * block(value, first + LAGS - lag).astype(F32)
         second = block(mixed, first) + dot((0.5 * total).astype(BF16), w_out[...])
         normed = rms_norm(second, gain_ffn[...]).astype(BF16)
-        hidden = w_in.shape[1]
-        for part in range(0, hidden, width):
-            x = dot(normed, w_in[:, part : part + width])
-            inner = x + x * jnp.tanh(x * (CURVE + 0.044715 * CURVE * (x * x)))
-            second += dot(inner.astype(BF16), w_down[part : part + width, :])
+        inner = []
+        for part in range(0, w_in.shape[1], width):
+            x = dot(normed, w_in[:, part : part + width]).astype(BF16)
+            curve = x * (BF16(CURVE) + BF16(0.044715 * CURVE) * (x * x))
+            inner.append(x + x * jnp.tanh(curve))
+        second += dot(jnp.concatenate(inner, axis=1), w_down[...])
         result[pl.ds(first, span)] = second.astype(BF16).reshape(span, firms, width)
 
     pass_on(0)
@@ -363,17 +364,6 @@
         @pl.loop(0, LAGS)
         def _(e):
             edge_copy(e).wait_send()
-
-
-def copy_kernel(source, result, sem):
-    copies = [
-        pltpu.make_async_copy(source.at[m], result.at[m], sem.at[m])
-        for m in range(source.shape[0])
-    ]
-    for copy in copies:
-        copy.start()
-    for copy in copies:
-        copy.wait()
 
 
 def body(groups, owners, features, supply_counts, bank_ids, sector_ids, bank_table, sector_table, *rest):
@@ -388,7 +378,7 @@
     hbm = pl.BlockSpec(memory_space=pltpu.HBM)
     hidden = weights[-1].shape[0]
     square = pltpu.VMEM((width, width), BF16)
-    out = pl.pallas_call(
+    return pl.pallas_call(
         functools.partial(kernel, groups, owners),
         out_shape=jax.ShapeDtypeStruct(block, BF16),
         in_specs=[hbm] * 2 + [vmem] * 4 + [hbm] * 7 + [vmem] * 2,
@@ -427,7 +417,7 @@
             dma((LAGS,)),
         ],
         compiler_params=pltpu.CompilerParams(
-            collective_id=0, has_side_effects=True, vmem_limit_bytes=50 * 1024 * 1024
+            collective_id=0, has_side_effects=True, vmem_limit_bytes=56 * 1024 * 1024
         ),
         cost_estimate=pl.CostEstimate(
             flops=2 * rows * width * (width * 5 + 3 * firms + 8 * width),
@@ -445,13 +435,6 @@
         gain_mix.reshape(1, width),
         gain_ffn.reshape(1, width),
     )
-    return pl.pallas_call(
-        copy_kernel,
-        out_shape=jax.ShapeDtypeStruct(block, BF16),
-        in_specs=[vmem],
-        out_specs=hbm,
-        scratch_shapes=[dma((months,))],
-    )(out)
 
 
 def solution(mesh):

time: 58.8 us -> 47.1 us (0.80)
  local copies, waits for them, and re-layouts: 12.9 us -> 2.26 us
  Pallas kernels: 45.3 us -> 44.6 us
    unnamed x30 -> x1, local copies, waits for them, and re-layouts: 12.9 us -> 2.26 us
    pallas_call x1 -> x0, Pallas kernels: 2.25 us -> none  [body(): pl.pallas_call(copy_kernel, out_shape=jax.ShapeDtypeStruct(block, BF16),...]
    pallas_call x1, Pallas kernels: 43.1 us -> 44.6 us  [body(): pl.pallas_call(functools.partial(kernel, groups, owners), out_shape=jax.S...]
where the time goes in v4:
time: 47.1 us; the launch traced here: 46.9 us
  Pallas kernels  44.6 us (95%)
  local copies, waits for them, and re-layouts  2.26 us (5%)
    pallas_call x1, Pallas kernels, body(): pl.pallas_call(functools.partial(kernel, groups, owners), out_shape=jax.S...  44.6 us
    unnamed x1, local copies, waits for them, and re-layouts  2.26 us

profile of v4, /device:TPU:4, one launch (start us, length us, event | category | flops | bytes accessed | tf_op | source)
XLA Modules:
  0.0 46.9 jit_solution(5432862455988657244)
XLA Ops:
  0.0 44.6 %shard_map.145 = bf16[8,256,256]{2,1,0:T(8,128)(2,1)} custom-call(bf16[8,256,256]{2,1,0:T(8,128)(2,1)} %features_hbm.1, s32[8,3,256,256]{3,2,1,0:T(8,128)} %bitcast.3, s32[8,256]{1,0:T(8,128)} %bank_ids.1, s32[8,256]{1,0:T(8,128)} %sector_ids.1, bf16[8,256]{1,0:T(8,128)(2,1)} %bank_table.1, bf16[4,256]{1,0:T(4,128)(2,1)} %sector_table.1, ...), custom_call_target="tpu_custom_call" | custom-call | flops 4294967296 | bytes 8388608 | tf_op jit(solution)/shard_map/pallas_call | solution.py:381
  44.6 2.3 %copy.17 = bf16[8,256,256]{2,1,0:T(8,128)(2,1)} copy(bf16[8,256,256]{2,1,0:T(8,128)(2,1)} %shard_map.145) | data formatting | bytes 2097152

commit v5 on v4

--- a/solution.py
+++ b/solution.py
@@ -45,7 +45,7 @@
     w_down_hbm,
     gain_mix,
     gain_ffn,
-    result,
+    result_hbm,
     features,
     w_supply,
     w_query,
@@ -54,6 +54,7 @@
     w_out,
     w_in,
     w_down,
+    result,
     counts,
     hub_own,
     hub,
@@ -68,6 +69,7 @@
     mixed,
     head_sum,
     load_sem,
+    result_sem,
     counts_sem,
     hub_send,
     hub_recv,
@@ -98,6 +100,9 @@
     def counts_copy(m):
         return pltpu.make_async_copy(counts_hbm.at[m], counts.at[m], counts_sem.at[m])
 
+    def result_copy(m):
+        return pltpu.make_async_copy(result.at[m], result_hbm.at[m], result_sem.at[m])
+
     loads = [
         pltpu.make_async_copy(src, dst, load_sem.at[i])
         for i, (src, dst) in enumerate(
@@ -310,6 +315,8 @@
             inner.append(x + x * jnp.tanh(curve))
         second += dot(jnp.concatenate(inner, axis=1), w_down[...])
         result[pl.ds(first, span)] = second.astype(BF16).reshape(span, firms, width)
+        for i in range(span):
+            result_copy(first + i).start()
 
     pass_on(0)
 
@@ -358,6 +365,8 @@
         def _():
             for h in range(HALVES):
                 relay_copy(m, h).wait_send()
+
+        result_copy(m).wait()
 
     @pl.when(has_after)
     def _():
@@ -382,7 +391,7 @@
         functools.partial(kernel, groups, owners),
         out_shape=jax.ShapeDtypeStruct(block, BF16),
         in_specs=[hbm] * 2 + [vmem] * 4 + [hbm] * 7 + [vmem] * 2,
-        out_specs=vmem,
+        out_specs=hbm,
         scratch_shapes=[
             pltpu.VMEM(block, BF16),
             square,
@@ -392,6 +401,7 @@
             square,
             pltpu.VMEM((width, hidden), BF16),
             pltpu.VMEM((hidden, width), BF16),
+            pltpu.VMEM(block, BF16),
             pltpu.VMEM((months, 3, firms, firms), jnp.int32),
             pltpu.VMEM((slot, width), F32),
             pltpu.VMEM((owners, slot, width), BF16),
@@ -406,6 +416,7 @@
             pltpu.VMEM(block, F32),
             pltpu.VMEM((width, width), BF16),
             dma((9,)),
+            dma((months,)),
             dma((months,)),
             dma((owners,)),
             dma((owners,)),

time: 47.1 us -> 46.8 us (level)
  no operation moved by 1% of the time
where the time goes in v5:
time: 46.8 us; the launch traced here: 46.6 us
  Pallas kernels  44.4 us (95%)
  local copies, waits for them, and re-layouts  2.26 us (5%)
    pallas_call x1, Pallas kernels, body(): pl.pallas_call(functools.partial(kernel, groups, owners), out_shape=jax.S...  44.4 us
    unnamed x1, local copies, waits for them, and re-layouts  2.26 us

profile of v5, /device:TPU:4, one launch (start us, length us, event | category | flops | bytes accessed | tf_op | source)
XLA Modules:
  0.0 46.6 jit_solution(13231795824434096561)
XLA Ops:
  0.0 44.4 %shard_map.145 = bf16[8,256,256]{2,1,0:T(8,128)(2,1)} custom-call(bf16[8,256,256]{2,1,0:T(8,128)(2,1)} %features_hbm.1, s32[8,3,256,256]{3,2,1,0:T(8,128)} %bitcast.3, s32[8,256]{1,0:T(8,128)} %bank_ids.1, s32[8,256]{1,0:T(8,128)} %sector_ids.1, bf16[8,256]{1,0:T(8,128)(2,1)} %bank_table.1, bf16[4,256]{1,0:T(4,128)(2,1)} %sector_table.1, ...), custom_call_target="tpu_custom_call" | custom-call | flops 4294967296 | bytes 8388608 | tf_op jit(solution)/shard_map/pallas_call | solution.py:390
  44.4 2.3 %copy.17 = bf16[8,256,256]{2,1,0:T(8,128)(2,1)} copy(bf16[8,256,256]{2,1,0:T(8,128)(2,1)} %shard_map.145) | data formatting | bytes 2097152

commit v6 on v5

--- a/solution.py
+++ b/solution.py
@@ -11,7 +11,7 @@
 HEADS = 4
 LAGS = 3
 AHEAD = 3
-HALVES = 2
+HALVES = 4
 CURVE = math.sqrt(2.0 / math.pi)
 MESH = pl.DeviceIdType.MESH
 F32 = jnp.float32

time: 46.8 us -> 47.5 us (1.015)
  Pallas kernels: 44.4 us -> 45 us
    pallas_call x1, Pallas kernels: 44.4 us -> 45 us  [body(): pl.pallas_call(functools.partial(kernel, groups, owners), out_shape=jax.S...]
where the time goes in v6:
time: 47.5 us; the launch traced here: 47.3 us
  Pallas kernels  45 us (95%)
  local copies, waits for them, and re-layouts  2.26 us (5%)
    pallas_call x1, Pallas kernels, body(): pl.pallas_call(functools.partial(kernel, groups, owners), out_shape=jax.S...  45 us
    unnamed x1, local copies, waits for them, and re-layouts  2.26 us

profile of v6, /device:TPU:4, one launch (start us, length us, event | category | flops | bytes accessed | tf_op | source)
XLA Modules:
  0.0 47.3 jit_solution(16310004992790765942)
XLA Ops:
  0.0 45.0 %shard_map.145 = bf16[8,256,256]{2,1,0:T(8,128)(2,1)} custom-call(bf16[8,256,256]{2,1,0:T(8,128)(2,1)} %features_hbm.1, s32[8,3,256,256]{3,2,1,0:T(8,128)} %bitcast.3, s32[8,256]{1,0:T(8,128)} %bank_ids.1, s32[8,256]{1,0:T(8,128)} %sector_ids.1, bf16[8,256]{1,0:T(8,128)(2,1)} %bank_table.1, bf16[4,256]{1,0:T(4,128)(2,1)} %sector_table.1, ...), custom_call_target="tpu_custom_call" | custom-call | flops 4294967296 | bytes 8388608 | tf_op jit(solution)/shard_map/pallas_call | solution.py:390
  45.0 2.3 %copy.17 = bf16[8,256,256]{2,1,0:T(8,128)(2,1)} copy(bf16[8,256,256]{2,1,0:T(8,128)(2,1)} %shard_map.145) | data formatting | bytes 2097152
